TPU v7x, 256 devices: a whole 4x4x8 slice. The times are simulated.
256 devices in a mesh: rows: 128 (over x, y_hi, z, core), heads: 2 (over y_lo).
Axes of the slice: x: 4, y: 4 (y_hi: 2, y_lo: 2; y = y_hi * 2 + y_lo), z: 8, core: 2. Of those that a mesh axis runs over, the one named last changes fastest.
Arguments:
- queries: bfloat16 [32768, 2048], P('rows', 'heads'), may hold values from -48 to 48
- keys: bfloat16 [32768, 2048], P('rows', 'heads'), may hold values from -24 to 24
- values: bfloat16 [32768, 2048], P('rows', 'heads'), may hold values from -6 to 6
- summary_cols: int32 [16], replicated, may hold values from 8 to 255, as said below
- w_out: bfloat16 [2048, 2048], P('heads'), may hold values from -1 to 1
Outputs:
- mixed: bfloat16 [32768, 2048], P('rows', 'heads')
Inputs may be any that keep to these rules, and one draw needn't show every extreme that they name: `summary_cols`: Rising; entry j lies in columns 16 * j + 8 to 16 * j + 15.
All inputs are finite; a program needn't handle non-finite values.
Results may differ from a plain program's by a relative error of at most 0.014.
Values may be sent and summed in bfloat16 or wider, within the bound.
A program may use at most 64 MiB of HBM per device.

v0:
```python
import math

import jax
import jax.numpy as jnp
from jax import lax
from jax.sharding import PartitionSpec as P

HEAD_DIM = 128
GRID_COLS = 256


negative = -1e30


def update(running, scores, allowed, block_v):
    peaks, totals, summed = running
    scores = jnp.where(allowed, scores, negative)
    new_peaks = jnp.maximum(peaks, jnp.max(scores, axis=-1))
    rescale = jnp.exp(peaks - new_peaks)
    weights = jnp.where(allowed, jnp.exp(scores - new_peaks[..., None]), 0.0)
    totals = rescale * totals + jnp.sum(weights, axis=-1)
    summed = rescale[..., None] * summed + jnp.einsum(
        "rchk,khe->rche", weights.astype(jnp.bfloat16), block_v, preferred_element_type=jnp.float32
    )
    return (new_peaks, totals, summed)


def on_device(queries, keys, values, summary_cols, w_out):
    n_rows = lax.axis_size("rows")
    width = queries.shape[1]
    heads_here = width // HEAD_DIM
    rows_here = queries.shape[0] // GRID_COLS
    rows_all = rows_here * n_rows
    sum_count = summary_cols.shape[0]
    inv_root = 1.0 / math.sqrt(HEAD_DIM)
    first_row = lax.axis_index("rows") * rows_here
    my_rows = first_row + jnp.arange(rows_here, dtype=jnp.int32)
    col_index = jnp.arange(GRID_COLS, dtype=jnp.int32)
    grid_q = queries.reshape(rows_here, GRID_COLS, heads_here, HEAD_DIM)
    grid_k = keys.reshape(rows_here, GRID_COLS, heads_here, HEAD_DIM)
    grid_v = values.reshape(rows_here, GRID_COLS, heads_here, HEAD_DIM)
    row_allowed = (col_index[None, :] < col_index[:, None])[None, :, None, :]
    scores = (
        jnp.einsum("rche,rkhe->rchk", grid_q, grid_k, preferred_element_type=jnp.float32) * inv_root
    )
    scores = jnp.where(row_allowed, scores, negative)
    peaks = jnp.max(scores, axis=-1)
    weights = jnp.where(row_allowed, jnp.exp(scores - peaks[..., None]), 0.0)
    totals = jnp.sum(weights, axis=-1)
    summed = jnp.einsum(
        "rchk,rkhe->rche", weights.astype(jnp.bfloat16), grid_v, preferred_element_type=jnp.float32
    )
    running = (peaks, totals, summed)
    sum_k = jnp.take(keys.reshape(rows_here, GRID_COLS, width), summary_cols, axis=1)
    sum_v = jnp.take(values.reshape(rows_here, GRID_COLS, width), summary_cols, axis=1)
    col_ok = summary_cols[None, :] != col_index[:, None]
    gathered_k, gathered_v = (
        lax.all_gather(sum_k, "rows", axis=0, tiled=True),
        lax.all_gather(sum_v, "rows", axis=0, tiled=True),
    )
    n_keys = gathered_k.shape[0]
    stride = math.gcd(n_keys, max(1, 512 // sum_count))

    def one_block(carry, block_no):
        offset = 0 + block_no * stride
        inner = block_no * stride
        block_k = lax.dynamic_slice_in_dim(gathered_k, inner, stride).reshape(
            stride * sum_count, heads_here, HEAD_DIM
        )
        block_v = lax.dynamic_slice_in_dim(gathered_v, inner, stride).reshape(
            stride * sum_count, heads_here, HEAD_DIM
        )
        key_rows = offset + jnp.arange(stride, dtype=jnp.int32)
        row_ok = key_rows[None, :] < my_rows[:, None]
        allowed = row_ok[:, None, :, None] & col_ok[None, :, None, :]
        allowed = allowed.reshape(rows_here, GRID_COLS, 1, stride * sum_count)
        block_scores = (
            jnp.einsum("rche,khe->rchk", grid_q, block_k, preferred_element_type=jnp.float32)
            * inv_root
        )
        return (update(carry, block_scores, allowed, block_v), None)

    result, unused = lax.scan(one_block, running, jnp.arange(n_keys // stride, dtype=jnp.int32))
    running = result
    row_index = jnp.arange(rows_all, dtype=jnp.int32)
    col_allowed = row_index[None, :] <= row_index[:, None]
    col_q, col_k, col_v = (
        lax.all_to_all(grid_q, "rows", split_axis=1, concat_axis=0, tiled=True),
        lax.all_to_all(grid_k, "rows", split_axis=1, concat_axis=0, tiled=True),
        lax.all_to_all(grid_v, "rows", split_axis=1, concat_axis=0, tiled=True),
    )
    col_scores = (
        jnp.einsum("rche,sche->chrs", col_q, col_k, preferred_element_type=jnp.float32) * inv_root
    )
    col_scores = jnp.where(col_allowed[None, None], col_scores, negative)
    col_peaks = jnp.max(col_scores, axis=-1)
    col_weights = jnp.where(
        col_allowed[None, None], jnp.exp(col_scores - col_peaks[..., None]), 0.0
    )
    col_totals = jnp.sum(col_weights, axis=-1)
    col_sum = jnp.einsum(
        "chrs,sche->rche",
        col_weights.astype(jnp.bfloat16),
        col_v,
        preferred_element_type=jnp.float32,
    )
    col_out = (col_sum / col_totals.transpose(2, 0, 1)[..., None]).astype(jnp.bfloat16)
    col_lse = (col_peaks + jnp.log(col_totals)).transpose(2, 0, 1)
    col_out, col_lse = (col_out, col_lse)
    back_out = lax.all_to_all(col_out, "rows", split_axis=0, concat_axis=1, tiled=True)
    back_lse = lax.all_to_all(col_lse, "rows", split_axis=0, concat_axis=1, tiled=True)
    back_out = back_out.astype(jnp.float32)
    peaks, totals, summed = running
    new_peaks = jnp.maximum(peaks, back_lse)
    rescale = jnp.exp(peaks - new_peaks)
    col_weight = jnp.exp(back_lse - new_peaks)
    totals = rescale * totals + col_weight
    summed = rescale[..., None] * summed + col_weight[..., None] * back_out
    attn = (summed / totals[..., None]).astype(jnp.bfloat16).reshape(rows_here * GRID_COLS, width)
    terms = jnp.dot(attn, w_out, preferred_element_type=jnp.float32)
    return lax.psum_scatter(terms.astype(jnp.bfloat16), "heads", scatter_dimension=1, tiled=True)


def solution(mesh):
    return jax.shard_map(
        on_device,
        mesh=mesh,
        in_specs=(
            P("rows", "heads"),
            P("rows", "heads"),
            P("rows", "heads"),
            P(),
            P("heads", None),
        ),
        out_specs=P("rows", "heads"),
        check_vma=False,
    )
```

profile of v0, /device:TPU:1, one launch (start us, length us, event | category | flops | bytes accessed | tf_op | source)
XLA Modules:
  0.0 326.6 jit_solution(8262378863054312165)
XLA Ops:
  6.5 0.7 compare_select_fusion
  7.9 1.7 gather_fusion
  9.7 1.7 gather_fusion.1
  11.4 0.7 bitcast_select_fusion.2
  12.2 0.7 all-gather.5.cloned.1.call-update
  12.9 1.2 copy.86
  14.1 1.1 copy.89
  15.2 16.4 %all-to-all-start = ((bf16[1,256,8,128]{3,2,0,1:T(8,128)(2,1)}), bf16[1,256,8,128]{3,2,0,1:T(8,128)(2,1)S(1)}, u32[]{:S(2)}, u32[]{:S(2)}) async-start(bf16[1,256,8,128]{3,2,0,1:T(8,128)(2,1)} %copy.89), calls=%async_computation | async-start | bytes 1048576 | tf_op jit(solution)/shard_map/all_to_all | solution.py:88
  31.6 0.9 copy.110
  32.5 20.9 %all-to-all-done = bf16[1,256,8,128]{3,2,0,1:T(8,128)(2,1)S(1)} async-done(((bf16[1,256,8,128]{3,2,0,1:T(8,128)(2,1)}), bf16[1,256,8,128]{3,2,0,1:T(8,128)(2,1)S(1)}, u32[]{:S(2)}, u32[]{:S(2)}) %all-to-all-start) | async-done | bytes 524320 | tf_op jit(solution)/shard_map/all_to_all | solution.py:88
  53.5 6.4 %all-to-all-start.1 = ((bf16[1,256,8,128]{3,2,0,1:T(8,128)(2,1)}), bf16[1,256,8,128]{3,2,0,1:T(8,128)(2,1)}, u32[]{:S(2)}, u32[]{:S(2)}) async-start(bf16[1,256,8,128]{3,2,0,1:T(8,128)(2,1)} %bitcast.57), calls=%async_computation.1 | async-start | bytes 1048576 | tf_op jit(solution)/shard_map/all_to_all | solution.py:89
  59.9 1.0 copy.88
  60.9 1.6 fusion.23
  62.5 2.9 convolution_bitcast_fusion.1
  65.4 1.6 copy.87
  67.0 2.0 copy.111
  68.9 11.9 %all-to-all-done.1 = bf16[1,256,8,128]{3,2,0,1:T(8,128)(2,1)} async-done(((bf16[1,256,8,128]{3,2,0,1:T(8,128)(2,1)}), bf16[1,256,8,128]{3,2,0,1:T(8,128)(2,1)}, u32[]{:S(2)}, u32[]{:S(2)}) %all-to-all-start.1) | async-done | bytes 524320 | tf_op jit(solution)/shard_map/all_to_all | solution.py:89
  80.8 6.4 %all-to-all-start.3 = ((bf16[1,256,8,128]{3,2,0,1:T(8,128)(2,1)}), bf16[1,256,8,128]{3,2,0,1:T(8,128)(2,1)}, u32[]{:S(2)}, u32[]{:S(2)}) async-start(bf16[1,256,8,128]{3,2,0,1:T(8,128)(2,1)} %bitcast.188), calls=%async_computation.3 | async-start | bytes 1048576 | tf_op jit(solution)/shard_map/all_to_all | solution.py:90
  87.8 1.7 fusion.65
  89.8 0.8 copy.92
  90.5 17.3 %all-to-all-done.3 = bf16[1,256,8,128]{3,2,0,1:T(8,128)(2,1)} async-done(((bf16[1,256,8,128]{3,2,0,1:T(8,128)(2,1)}), bf16[1,256,8,128]{3,2,0,1:T(8,128)(2,1)}, u32[]{:S(2)}, u32[]{:S(2)}) %all-to-all-start.3) | async-done | bytes 524320 | tf_op jit(solution)/shard_map/all_to_all | solution.py:90
  107.9 5.5 %all-to-all-start.2 = ((f32[128,2,8]{2,1,0:T(2,128)}), f32[128,2,8]{2,1,0:T(2,128)S(1)}, u32[]{:S(2)}, u32[]{:S(2)}) async-start(f32[128,2,8]{2,1,0:T(2,128)} %copy.92), calls=%async_computation.2 | async-start | bytes 262144 | tf_op jit(solution)/shard_map/all_to_all | solution.py:111
  113.4 1.7 fusion.28
  115.0 1.2 copy.100
  116.2 11.6 %all-to-all-done.2 = f32[128,2,8]{2,1,0:T(2,128)S(1)} async-done(((f32[128,2,8]{2,1,0:T(2,128)}), f32[128,2,8]{2,1,0:T(2,128)S(1)}, u32[]{:S(2)}, u32[]{:S(2)}) %all-to-all-start.2) | async-done | bytes 8224 | tf_op jit(solution)/shard_map/all_to_all | solution.py:111
  127.8 6.6 %all-to-all-start.4 = ((bf16[128,2,8,128]{3,2,1,0:T(8,128)(2,1)}), bf16[128,2,8,128]{3,2,1,0:T(8,128)(2,1)}, u32[]{:S(2)}, u32[]{:S(2)}) async-start(bf16[128,2,8,128]{3,2,1,0:T(8,128)(2,1)} %copy.100), calls=%async_computation.4 | async-start | bytes 1048576 | tf_op jit(solution)/shard_map/all_to_all | solution.py:110
  134.5 3.3 %all-gather.3.cloned.1.call-done = bf16[128,16,1024]{2,1,0:T(8,128)(2,1)} async-done(((bf16[1,16,1024]{2,1,0:T(8,128)(2,1)}), bf16[128,16,1024]{2,1,0:T(8,128)(2,1)}) %all-gather.3.cloned.1.call-update) | async-done | bytes 4194320 | tf_op jit(solution)/shard_map/all_gather | solution.py:58
  137.8 119.1 %all-gather.5.cloned.1.call-done = bf16[128,16,1024]{2,1,0:T(8,128)(2,1)} async-done(((bf16[1,16,1024]{2,1,0:T(8,128)(2,1)}), bf16[128,16,1024]{2,1,0:T(8,128)(2,1)}) %all-gather.5.cloned.1.call-update) | async-done | bytes 4194320 | tf_op jit(solution)/shard_map/all_gather | solution.py:59
  256.9 34.0 %while.15 = (s32[]{:T(128)}, f32[1,256,8]{1,2,0:T(8,128)S(1)}, f32[1,256,8]{1,2,0:T(8,128)S(1)}, f32[1,256,8,128]{1,3,2,0:T(8,128)S(1)}, s32[4]{0:T(128)S(1)}, /...) while((s32[]{:T(128)}, f32[1,256,8]{1,2,0:T(8,128)S(1)}, ...), condition=%wide.region_5.7_spmd.clone, body=%wide.region_2.6_spmd.clone.sunk | while | flops 551168064 | bytes 26356044 | solution.py:83
  258.2 1.7 constant_dynamic-slice_fusion.3
  260.6 1.9 fusion.78
  262.7 1.6 fusion.81
  264.4 1.0 fusion.80
  266.7 1.7 constant_dynamic-slice_fusion.3
  269.1 1.9 fusion.78
  271.2 1.6 fusion.81
  272.9 1.0 fusion.80
  275.2 1.7 constant_dynamic-slice_fusion.3
  277.6 1.9 fusion.78
  279.7 1.6 fusion.81
  281.4 1.0 fusion.80
  283.7 1.7 constant_dynamic-slice_fusion.3
  286.1 1.9 fusion.78
  288.2 1.6 fusion.81
  289.9 1.0 fusion.80
  291.8 1.9 fusion.33
  293.7 4.4 %convolution_convert_fusion = bf16[256,2048]{1,0:T(8,128)(2,1)} fusion(bf16[1024,2048]{1,0:T(8,128)(2,1)} %param.13, bf16[32,8,8,128]{3,2,1,0:T(8,128)(2,1)S(1)} %bitcast.192), kind=kOutput, calls=%fused_computation.29 | convolution fusion | flops 1074266112 | bytes 5767168 | tf_op jit(solution)/shard_map/dot_general | solution.py:120
  298.2 21.9 %reduce-scatter.2.cloned.1.call-done = bf16[256,1024]{1,0:T(8,128)(2,1)} async-done(((bf16[256,2048]{1,0:T(8,128)(2,1)}), bf16[256,1024]{1,0:T(8,128)(2,1)}) %reduce-scatter.2.cloned.1.call-update) | async-done | bytes 524304 | tf_op jit(solution)/shard_map/reduce_scatter | solution.py:121
  (70 shorter events, 8.6 us)
Async XLA Ops:
  6.5 25.1 %copy-start = (bf16[256,1024]{1,0:T(8,128)(2,1)S(1)}, bf16[256,1024]{1,0:T(8,128)(2,1)}, u32[]{:S(2)}) copy-start(bf16[256,1024]{1,0:T(8,128)(2,1)} %param.10) | copy-start | bytes 1572868
  6.5 131.3 %all-gather.3.cloned.1.call-start = ((), (), s32[]{:S(2)}) async-start(), calls=%async_computation.6 | async-start | bytes 4227072 | tf_op jit(solution)/shard_map/all_gather | solution.py:58
  12.1 244.8 %all-gather.5.cloned.1.call-start = ((), (), s32[]{:S(2)}) async-start(), calls=%async_computation.7 | async-start | bytes 4227072 | tf_op jit(solution)/shard_map/all_gather | solution.py:59
  15.2 38.3 %all-to-all-start = ((bf16[1,256,8,128]{3,2,0,1:T(8,128)(2,1)}), bf16[1,256,8,128]{3,2,0,1:T(8,128)(2,1)S(1)}, u32[]{:S(2)}, u32[]{:S(2)}) async-start(bf16[1,256,8,128]{3,2,0,1:T(8,128)(2,1)} %copy.89), calls=%async_computation | async-start | bytes 1048576 | tf_op jit(solution)/shard_map/all_to_all | solution.py:88
  53.5 7.4 %copy-start.1 = (bf16[1,256,8,128]{3,2,0,1:T(8,128)(2,1)}, bf16[1,256,8,128]{3,2,0,1:T(8,128)(2,1)S(1)}, u32[]{:S(2)}) copy-start(bf16[1,256,8,128]{3,2,0,1:T(8,128)(2,1)S(1)} %all-to-all-done) | copy-start | bytes 1572868
  53.5 27.4 %all-to-all-start.1 = ((bf16[1,256,8,128]{3,2,0,1:T(8,128)(2,1)}), bf16[1,256,8,128]{3,2,0,1:T(8,128)(2,1)}, u32[]{:S(2)}, u32[]{:S(2)}) async-start(bf16[1,256,8,128]{3,2,0,1:T(8,128)(2,1)} %bitcast.57), calls=%async_computation.1 | async-start | bytes 1048576 | tf_op jit(solution)/shard_map/all_to_all | solution.py:89
  80.8 27.1 %all-to-all-start.3 = ((bf16[1,256,8,128]{3,2,0,1:T(8,128)(2,1)}), bf16[1,256,8,128]{3,2,0,1:T(8,128)(2,1)}, u32[]{:S(2)}, u32[]{:S(2)}) async-start(bf16[1,256,8,128]{3,2,0,1:T(8,128)(2,1)} %bitcast.188), calls=%async_computation.3 | async-start | bytes 1048576 | tf_op jit(solution)/shard_map/all_to_all | solution.py:90
  89.7 167.2 %copy-start.2 = (s32[16]{0:T(128)S(1)}, s32[16]{0:T(128)}, u32[]{:S(2)}) copy-start(s32[16]{0:T(128)} %param.12) | copy-start | bytes 196
  107.9 19.9 %all-to-all-start.2 = ((f32[128,2,8]{2,1,0:T(2,128)}), f32[128,2,8]{2,1,0:T(2,128)S(1)}, u32[]{:S(2)}, u32[]{:S(2)}) async-start(f32[128,2,8]{2,1,0:T(2,128)} %copy.92), calls=%async_computation.2 | async-start | bytes 262144 | tf_op jit(solution)/shard_map/all_to_all | solution.py:111
  127.8 164.0 %all-to-all-start.4 = ((bf16[128,2,8,128]{3,2,1,0:T(8,128)(2,1)}), bf16[128,2,8,128]{3,2,1,0:T(8,128)(2,1)}, u32[]{:S(2)}, u32[]{:S(2)}) async-start(bf16[128,2,8,128]{3,2,1,0:T(8,128)(2,1)} %copy.100), calls=%async_computation.4 | async-start | bytes 1048576 | tf_op jit(solution)/shard_map/all_to_all | solution.py:110
  134.4 185.6 %reduce-scatter.2.cloned.1.call-start = ((), (), s32[]{:S(2)}) async-start(), calls=%async_computation.8 | async-start | bytes 1572864 | tf_op jit(solution)/shard_map/reduce_scatter | solution.py:121
Sparse Core Ops, SparseCore 0:
  12.2 125.5 all-gather.2
  141.6 115.2 all-gather.4
  298.3 21.7 reduce-scatter.1
where the time goes:
time: 328 us; the launch traced here: 327 us
  waiting for transfers between devices  207 us (63%)
  starting transfers between devices  41.4 us (13%)
  matrix products  26.2 us (8%)
  local copies, waits for them, and re-layouts  26.1 us (8%)
  between operations  13.3 us (4%)
  other arithmetic  9.84 us (3%)
    all_gather x1, waiting for transfers between devices, on_device(): lax.all_gather(sum_v, 'rows', axis=0, tiled=True)  119 us
    reduce_scatter x1, waiting for transfers between devices, on_device(): lax.psum_scatter(terms.astype(jnp.bfloat16), 'heads', scatter_dimension=1...  21.9 us
    all_to_all x1, waiting for transfers between devices, on_device(): lax.all_to_all(grid_q, 'rows', split_axis=1, concat_axis=0, tiled=True)  20.9 us
    all_to_all x1, waiting for transfers between devices, on_device(): lax.all_to_all(grid_v, 'rows', split_axis=1, concat_axis=0, tiled=True)  17.3 us
    all_to_all x1, starting transfers between devices, on_device(): lax.all_to_all(grid_q, 'rows', split_axis=1, concat_axis=0, tiled=True)  16.4 us
    all_to_all x1, waiting for transfers between devices, on_device(): lax.all_to_all(grid_k, 'rows', split_axis=1, concat_axis=0, tiled=True)  11.9 us
    all_to_all x1, waiting for transfers between devices, on_device(): lax.all_to_all(col_lse, 'rows', split_axis=0, concat_axis=1, tiled=True)  11.6 us
    dot_general x4, matrix products, one_block(): jnp.einsum('rche,khe->rchk', grid_q, block_k, preferred_element_type=jnp....  7.47 us
  transfers between devices with their start and end apart: 8, of which 7 were waited for; matrix products, arithmetic and copies ran while one was open for 15% of the time, Pallas kernels for 0%

commit v1 on v0

v1 whole, which is shorter than its diff:
```python
import math

import jax
import jax.numpy as jnp
from jax import lax
from jax.experimental import pallas as pl
from jax.experimental.pallas import tpu as pltpu
from jax.sharding import PartitionSpec as P

HEAD_DIM = 128
COLS = 256
HALF = 128
SUMS = 16
NZ = 8
NG = 8
MESH = pl.DeviceIdType.MESH
BF, F32 = jnp.bfloat16, jnp.float32
BIG = 1e30
TO_LOG2 = math.log2(math.e) / math.sqrt(HEAD_DIM)


def nt(a, b):
    return lax.dot_general(a, b, (((1,), (1,)), ((), ())), preferred_element_type=F32)


def nn(a, b):
    return jnp.dot(a, b, preferred_element_type=F32)


def iota(shape, dim):
    return lax.broadcasted_iota(jnp.int32, shape, dim)


def body(cols_ref, q_hbm, k_hbm, v_hbm, w_hbm, o_ref, zbuf, pbuf, ybuf, obuf, rbuf, cbuf, abuf, home, wbuf,
         kvl, ssel, sz, sg, qb, ekey, perm, lsrc, lbuf, acc, mx, tot, own, xsend, xrecv,
         zss, zrs, gss, grs, pss, prs, rss, rrs, lss, lrs, ass, ars, xss, xrs, loc):
    me = lax.axis_index("rows")
    t = lax.axis_index("heads")
    c = me % 2
    z = (me // 2) % NZ
    g = me // (2 * NZ)
    p = g * 2 + c

    def row_id(gg, zz, cc):
        return (gg * NZ + zz) * 2 + cc

    def z_mate(s):
        zz = (z + s) % NZ
        return zz, {"rows": row_id(g, zz, c)}

    def remote(src, dst, ssem, rsem, device):
        return pltpu.make_async_remote_copy(
            src_ref=src, dst_ref=dst, send_sem=ssem, recv_sem=rsem, device_id=device, device_id_type=MESH
        )

    def drain(ref, sem):
        pltpu.make_async_copy(ref, ref, sem).wait()

    hbm = (q_hbm, k_hbm, v_hbm)
    kv_loads = [pltpu.make_async_copy(hbm[1 + a], kvl.at[a], loc.at[a]) for a in range(2)]
    for load in kv_loads:
        load.start()
    w_load = pltpu.make_async_copy(w_hbm, wbuf, loc.at[2])

    barrier = pltpu.get_barrier_semaphore()

    @pl.loop(1, NZ)
    def _(s):
        pl.semaphore_signal(barrier, inc=1, device_id=z_mate(s)[1], device_id_type=MESH)

    @pl.loop(1, 2 * NG)
    def _(s):
        d = (p + s) % (2 * NG)
        pl.semaphore_signal(barrier, inc=1, device_id={"rows": row_id(d // 2, z, d % 2)}, device_id_type=MESH)

    pl.semaphore_signal(barrier, inc=1, device_id={"heads": 1 - t}, device_id_type=MESH)

    lane1 = iota((1, HEAD_DIM), 1)
    sub16 = iota((SUMS, COLS), 0)
    as_row = jnp.full((1, HEAD_DIM), -1, jnp.int32)
    as_col = jnp.full((SUMS, COLS), -1, jnp.int32)
    for j in range(SUMS):
        as_row = jnp.where(lane1 == j, cols_ref[j], as_row)
        as_col = jnp.where(sub16 == j, cols_ref[j], as_col)
    pick = jnp.where(iota((SUMS, COLS), 1) == as_col, 1.0, 0.0).astype(BF)

    for load in kv_loads:
        load.wait()
    for a in range(2):
        ssel[a] = nn(pick, kvl[a]).astype(BF)
    pl.semaphore_wait(barrier, NZ - 1 + 2 * NG - 1 + 1)

    def head_lanes(zz):
        return pl.ds(pl.multiple_of(zz * HEAD_DIM, HEAD_DIM), HEAD_DIM)

    pltpu.make_async_copy(ssel.at[:, :, head_lanes(z)], sz.at[:, z], zrs.at[6]).start()

    @pl.loop(1, NZ)
    def _(s):
        zz, device = z_mate(s)
        remote(ssel.at[:, :, head_lanes(zz)], sz.at[:, z], zss.at[6], zrs.at[6], device).start()

    for h in range(2):
        for a in range(3):
            ch = h * 3 + a
            rows = pl.ds(h * HALF, HALF)
            pltpu.make_async_copy(hbm[a].at[rows, head_lanes(z)], zbuf.at[a, z, rows], zrs.at[ch]).start()

            @pl.loop(1, NZ)
            def _(s):
                zz, device = z_mate(s)
                remote(hbm[a].at[rows, head_lanes(zz)], zbuf.at[a, z, rows], zss.at[ch], zrs.at[ch], device).start()

    w_load.start()

    lane = iota((COLS, HEAD_DIM), 1)
    not_own = jnp.where(iota((COLS, HEAD_DIM), 0) == as_row, -BIG, 0.0)
    for zz in range(NZ):
        pos = lane - SUMS
        kz, cc = pos % NZ, pos // NZ
        later = (kz > zz) | ((kz == zz) & (cc >= c))
        in_lanes = (pos >= 0) & (pos < 2 * NZ)
        qb[zz] = jnp.where(in_lanes & later, -BIG, not_own).astype(BF)
    key = iota((COLS, HEAD_DIM), 0)
    for_j = lane == key % SUMS
    for_row = lane == SUMS + key // SUMS
    ekey[0] = jnp.where(for_j, 1.0, 0.0).astype(BF)
    ekey[1] = jnp.where(for_j | for_row, 1.0, 0.0).astype(BF)
    out_i, in_i = iota((COLS, COLS), 0), iota((COLS, COLS), 1)
    perm[...] = jnp.where((out_i // 16 == in_i % 16) & (out_i % 16 == in_i // 16), 1.0, 0.0).astype(BF)
    eye = jnp.where(iota((HALF, HALF), 0) == iota((HALF, HALF), 1), 1.0, 0.0).astype(BF)
    ones = jnp.ones((16, COLS), BF)
    acc[...] = jnp.zeros_like(acc)
    mx[...] = jnp.full_like(mx, -BIG)
    tot[...] = jnp.zeros_like(tot)

    drain(sz, zrs.at[6])
    pltpu.make_async_copy(sz, sg.at[:, p], grs).start()

    @pl.loop(1, 2 * NG)
    def _(s):
        d = (p + s) % (2 * NG)
        remote(sz, sg.at[:, p], gss, grs, {"rows": row_id(d // 2, z, d % 2)}).start()

    def forward(a, h):
        chunk = zbuf.at[a, :, pl.ds(h * HALF, HALF)]
        drain(chunk, zrs.at[h * 3 + a])

        def part(gg):
            return zbuf.at[a, :, pl.ds(pl.multiple_of(h * HALF + gg * 16, 16), 16)]

        @pl.loop(1, NG)
        def _(s):
            gg = (g + s) % NG
            remote(part(gg), pbuf.at[a, p], pss.at[a, h], prs.at[a], {"rows": row_id(gg, z, h)}).start()

        @pl.when(c == h)
        def _():
            pltpu.make_async_copy(part(g), pbuf.at[a, p], prs.at[a]).start()

        @pl.when(c != h)
        def _():
            remote(part(g), pbuf.at[a, p], pss.at[a, h], prs.at[a], {"rows": row_id(g, z, h)}).start()

    def update(h, i, lanes, s, vt):
        old = mx[h, i, :1, lanes]
        new = jnp.maximum(old, jnp.max(s, axis=0, keepdims=True))
        shrink = jnp.exp2(old - new)
        got = nn(vt, jnp.exp2(s - new).astype(BF))
        acc[h, i, :, lanes] = acc[h, i, :, lanes] * shrink + got[:HEAD_DIM]
        tot[h, i, :1, lanes] = tot[h, i, :1, lanes] * shrink + got[HEAD_DIM : HEAD_DIM + 1]
        mx[h, i, :1, lanes] = new

    def summary(h):
        @pl.loop(0, g + 1)
        def _(gg):
            keys = sg[0, pl.ds(2 * gg, 2)].reshape(COLS, HEAD_DIM)
            vals = sg[1, pl.ds(2 * gg, 2)].reshape(COLS, HEAD_DIM)
            keys = jnp.concatenate([keys, ekey[(gg == g).astype(jnp.int32)]], axis=1)
            vt = jnp.concatenate([nt(eye, vals).astype(BF), ones], axis=0)
            for i in range(NZ // 2):
                rows = (slice(2 * i, 2 * i + 2), slice(h * HALF, (h + 1) * HALF))
                qs = jnp.concatenate(
                    [zbuf[0, rows[0], rows[1]].reshape(COLS, HEAD_DIM), qb[rows[0], rows[1]].reshape(COLS, HEAD_DIM)],
                    axis=1,
                )
                update(h, i, slice(0, COLS), nt(keys, qs) * TO_LOG2, vt)

    def near(h):
        n = HALF * (h + 1)
        before = iota((n, HALF), 0) < iota((n, HALF), 1) + h * HALF

        @pl.loop(0, NZ // 2)
        def _(i):
            for e in range(2):
                zz = 2 * i + e
                s = nt(zbuf[1, zz, :n], zbuf[0, zz, h * HALF : (h + 1) * HALF]) * TO_LOG2
                s = jnp.where(before, s, -BIG)
                vt = jnp.concatenate([nt(eye, zbuf[2, zz, :n]).astype(BF), ones[:, :n]], axis=0)
                update(h, i, slice(e * HALF, (e + 1) * HALF), s, vt)

    def column(h):
        @pl.when(c == h)
        def _():
            for a in range(3):
                drain(pbuf.at[a], prs.at[a])

                @pl.loop(0, NG)
                def _(gg):
                    y = nn(perm[...], pbuf[a, pl.ds(2 * gg, 2)].reshape(COLS, HEAD_DIM))
                    ybuf[a, :, gg] = y.astype(BF).reshape(16, 16, HEAD_DIM)

            def row_of(i):
                return (i // 16) * 16 + (i % 8) * 2 + (i // 8) % 2

            sh = (HALF, HALF)
            causal = row_of(iota(sh, 1)) <= row_of(iota(sh, 0))
            own_lane = iota(sh, 1) - g * 16
            one = jnp.ones(sh, BF)

            @pl.loop(0, 16)
            def _(i):
                qc, kc, vc = (ybuf[a, i].reshape(HALF, HEAD_DIM) for a in range(3))
                s = jnp.where(causal, nt(qc, kc) * TO_LOG2, -BIG)
                peak = jnp.max(s, axis=1, keepdims=True)
                w = jnp.exp2(s - peak).astype(BF)
                got = nn(w, jnp.concatenate([vc, one], axis=1))
                total = got[:, HEAD_DIM:]
                obuf[i] = (got[:, :HEAD_DIM] / total).astype(BF).reshape(NG, 16, HEAD_DIM)
                lse = peak + jnp.log2(total)
                lsrc[...] = jnp.where(own_lane == i, lse, jnp.where(i == 0, 0.0, lsrc[...]))

            def give_back(gg):
                x = nn(perm[...], obuf[:, gg].reshape(COLS, HEAD_DIM))
                rbuf[pl.ds(2 * gg, 2)] = x.astype(BF).reshape(2, NZ, 16, HEAD_DIM)

            def send_back(gg, cc):
                d = gg * 2 + cc
                device = {"rows": row_id(gg, z, cc)}
                tile = lsrc.at[pl.ds(pl.multiple_of(d * NZ, NZ), NZ)]
                remote(rbuf.at[d], cbuf.at[h, g], rss, rrs.at[h], device).start()
                remote(tile, lbuf.at[h, g], lss, lrs.at[h], device).start()

            @pl.loop(1, NG)
            def _(s):
                gg = (g + s) % NG
                give_back(gg)
                for cc in range(2):
                    send_back(gg, cc)

            give_back(g)
            send_back(g, 1 - h)
            pltpu.make_async_copy(rbuf.at[p], cbuf.at[h, g], rrs.at[h]).start()
            tile = lsrc.at[pl.ds(pl.multiple_of(p * NZ, NZ), NZ)]
            pltpu.make_async_copy(tile, lbuf.at[h, g], lrs.at[h]).start()

    def merge(h):
        drain(cbuf.at[h], rrs.at[h])
        drain(lbuf.at[h], lrs.at[h])
        lse_all = jnp.sum(lbuf[h], axis=0)
        rows = slice(h * HALF, (h + 1) * HALF)
        for zz in range(NZ):
            lanes = slice((zz % 2) * HALF, (zz % 2 + 1) * HALF)
            lse = lse_all[zz : zz + 1]
            m = mx[h, zz // 2, :1, lanes]
            peak = jnp.maximum(m, lse)
            near_w = jnp.exp2(m - peak)
            col_w = jnp.exp2(lse - peak)
            inv = 1.0 / (tot[h, zz // 2, :1, lanes] * near_w + col_w)
            col_t = nt(eye, cbuf[h, :, zz].reshape(HALF, HEAD_DIM))
            out_t = acc[h, zz // 2, :, lanes] * (near_w * inv) + col_t * (col_w * inv)
            abuf[zz, rows] = nt(eye, out_t.astype(BF)).astype(BF)
        rows = pl.ds(h * HALF, HALF)
        pltpu.make_async_copy(abuf.at[z, rows], home.at[rows, head_lanes(z)], ars.at[h]).start()

        @pl.loop(1, NZ)
        def _(s):
            zz, device = z_mate(s)
            remote(abuf.at[zz, rows], home.at[rows, head_lanes(z)], ass.at[h], ars.at[h], device).start()

    width = NZ * HEAD_DIM

    def project(h):
        rows = pl.ds(h * HALF, HALF)
        drain(home.at[rows], ars.at[h])
        theirs = pl.ds(pl.multiple_of((1 - t) * width, width), width)
        ours = pl.ds(pl.multiple_of(t * width, width), width)
        xsend[h] = nn(home[rows], wbuf[:, theirs]).astype(BF)
        remote(xsend.at[h], xrecv.at[h], xss.at[h], xrs.at[h], {"heads": 1 - t}).start()
        own[h] = nn(home[rows], wbuf[:, ours])

    def finish(h):
        drain(xrecv.at[h], xrs.at[h])
        o_ref[pl.ds(h * HALF, HALF)] = (own[h] + xrecv[h].astype(F32)).astype(BF)

    for a in range(3):
        forward(a, 0)
    drain(sg, grs)
    near(0)
    column(0)
    forward(0, 1)
    summary(0)
    forward(1, 1)
    merge(0)
    summary(1)
    forward(2, 1)
    near(1)
    column(1)
    w_load.wait()
    project(0)
    merge(1)
    project(1)
    finish(0)
    finish(1)

    drain(sz.at[:, pl.ds(0, NZ - 1)], zss.at[6])
    drain(sg.at[:, pl.ds(0, 2 * NG - 1)], gss)
    for h in range(2):
        rows = pl.ds(h * HALF, HALF)
        for a in range(3):
            drain(zbuf.at[a, pl.ds(0, NZ - 1), rows], zss.at[h * 3 + a])

            @pl.when(c == h)
            def _():
                drain(pbuf.at[a, pl.ds(0, NG - 1)], pss.at[a, h])

            @pl.when(c != h)
            def _():
                drain(pbuf.at[a, pl.ds(0, NG)], pss.at[a, h])

        drain(abuf.at[pl.ds(0, NZ - 1), rows], ass.at[h])
        drain(xsend.at[h], xss.at[h])
    drain(rbuf.at[pl.ds(0, 2 * NG - 1)], rss)
    drain(lsrc.at[pl.ds(0, (2 * NG - 1) * NZ)], lss)


def on_device(queries, keys, values, summary_cols, w_out):
    width = queries.shape[1]
    any_space = pl.BlockSpec(memory_space=pl.ANY)
    dma = pltpu.SemaphoreType.DMA
    vmem = pltpu.VMEM
    e = HEAD_DIM
    return pl.pallas_call(
        body,
        out_shape=jax.ShapeDtypeStruct(queries.shape, BF),
        in_specs=[pl.BlockSpec(memory_space=pltpu.SMEM)] + [any_space] * 4,
        out_specs=pl.BlockSpec(memory_space=pltpu.VMEM),
        scratch_shapes=[
            vmem((3, NZ, COLS, e), BF),
            vmem((3, 2 * NG, NZ, 16, e), BF),
            vmem((3, 16, NG, 16, e), BF),
            vmem((16, NG, 16, e), BF),
            vmem((2 * NG, NZ, 16, e), BF),
            vmem((2, NG, NZ, 16, e), BF),
            vmem((NZ, COLS, e), BF),
            vmem((COLS, width), BF),
            vmem(w_out.shape, BF),
            vmem((2, COLS, width), BF),
            vmem((2, SUMS, width), BF),
            vmem((2, NZ, SUMS, e), BF),
            vmem((2, 2 * NG, NZ, SUMS, e), BF),
            vmem((NZ, COLS, e), BF),
            vmem((2, COLS, e), BF),
            vmem((COLS, COLS), BF),
            vmem((HALF, e), F32),
            vmem((2, NG, NZ, e), F32),
            vmem((2, NZ // 2, e, COLS), F32),
            vmem((2, NZ // 2, 8, COLS), F32),
            vmem((2, NZ // 2, 8, COLS), F32),
            vmem((2, HALF, width), F32),
            vmem((2, HALF, width), BF),
            vmem((2, HALF, width), BF),
            dma((7,)), dma((7,)),
            dma, dma,
            dma((3, 2)), dma((3,)),
            dma, dma((2,)),
            dma, dma((2,)),
            dma((2,)), dma((2,)),
            dma((2,)), dma((2,)),
            dma((3,)),
        ],
        name="strided_attention",
        compiler_params=pltpu.CompilerParams(
            collective_id=0, has_side_effects=True, vmem_limit_bytes=48 * 1024 * 1024
        ),
    )(summary_cols, queries, keys, values, w_out)


def solution(mesh):
    return jax.shard_map(
        on_device,
        mesh=mesh,
        in_specs=(P("rows", "heads"), P("rows", "heads"), P("rows", "heads"), P(), P("heads", None)),
        out_specs=P("rows", "heads"),
        check_vma=False,
    )
```

time: 328 us -> 108 us (0.33)
  waiting for transfers between devices: 207 us -> 0 us
  Pallas kernels: 0 us -> 102 us
  starting transfers between devices: 41.4 us -> 0 us
  matrix products: 26.2 us -> 0 us
  local copies, waits for them, and re-layouts: 26.1 us -> 4.57 us
  between operations: 13.3 us -> 0.01 us
  other arithmetic: 9.84 us -> 0 us
    all_gather x2 -> x0, waiting for transfers between devices: 122 us -> none  [the longest x1 119 us: on_device(): lax.all_gather(sum_v, 'rows', axis=0, tiled=True)]
    pallas_call x0 -> x1, Pallas kernels: none -> 102 us  [on_device(): pl.pallas_call(body, out_shape=jax.ShapeDtypeStruct(queries.shape, BF), i...]
    all_to_all x5 -> x0, waiting for transfers between devices: 61.7 us -> none  [the longest x1 20.9 us: on_device(): lax.all_to_all(grid_q, 'rows', split_axis=1, concat_axis=0, tiled=True)]
    all_to_all x5 -> x0, starting transfers between devices: 41.3 us -> none  [the longest x1 16.4 us: on_device(): lax.all_to_all(grid_q, 'rows', split_axis=1, concat_axis=0, tiled=True)]
    dot_general x13 -> x0, matrix products: 26.2 us -> none  [the longest x4 7.47 us: one_block(): jnp.einsum('rche,khe->rchk', grid_q, block_k, preferred_element_type=jnp....]
    reduce_scatter x1 -> x0, waiting for transfers between devices: 21.9 us -> none  [on_device(): lax.psum_scatter(terms.astype(jnp.bfloat16), 'heads', scatter_dimension=1...]
    dynamic_slice x8 -> x0, local copies, waits for them, and re-layouts: 9.28 us -> none  [the longest x4 6.88 us: one_block(): lax.dynamic_slice_in_dim(gathered_v, inner, stride)]
    reduce_sum x6 -> x0, other arithmetic: 4.75 us -> none  [the longest x4 4.03 us: update(): totals = rescale * totals + jnp.sum(weights, axis=-1)]
  transfers between devices with their start and end apart: 8 -> 0, of which waited for: 7 -> 0; matrix products, arithmetic and copies ran while one was open for 15% -> 0% of each run, Pallas kernels for 0% -> 0%
where the time goes in v1:
time: 108 us; the launch traced here: 106 us
  Pallas kernels  102 us (94%)
  local copies, waits for them, and re-layouts  4.57 us (4%)
    pallas_call x1, Pallas kernels, on_device(): pl.pallas_call(body, out_shape=jax.ShapeDtypeStruct(queries.shape, BF), i...  102 us
    unnamed x9, local copies, waits for them, and re-layouts  4.57 us

profile of v1, /device:TPU:1, one launch (start us, length us, event | category | flops | bytes accessed | tf_op | source)
XLA Modules:
  0.0 106.3 jit_solution(18016281562416052579)
XLA Ops:
  0.0 0.0 copy-start
  0.0 1.0 copy-done
  1.0 0.0 copy-start.1
  1.0 1.0 copy-done.1
  2.1 0.0 copy-start.2
  2.1 1.0 copy-done.2
  3.1 0.0 copy-start.3
  3.1 0.7 copy-done.3
  3.8 101.7 %strided_attention.1 = bf16[256,1024]{1,0:T(8,128)(2,1)S(1)} custom-call(s32[16]{0:T(128)S(1)} %copy-done.3, bf16[256,1024]{1,0:T(8,128)(2,1)S(1)} %copy-done, bf16[256,1024]{1,0:T(8,128)(2,1)S(1)} %copy-done.1, bf16[256,1024]{1,0:T(8,128)(2,1)S(1)} %copy-done.2, bf16[1024,2048]{1,0:T(8,128)(2,1)} %w_hbm.1), custom_call_target="tpu_custom_call" | custom-call | tf_op jit(solution)/shard_map/strided_attention/pallas_call | solution.py:343
  105.5 0.8 copy.7
Async XLA Ops:
  0.0 1.0 copy-start
  1.0 1.0 copy-start.1
  2.1 1.0 copy-start.2
  3.1 0.7 copy-start.3

commit v2 on v1

v2 whole, which is shorter than its diff:
```python
import math

import jax
import jax.numpy as jnp
from jax import lax
from jax.experimental import pallas as pl
from jax.experimental.pallas import tpu as pltpu
from jax.sharding import PartitionSpec as P

HEAD_DIM = 128
COLS = 256
SUMS = 16
NZ = 8
NG = 8
BLOCK = 16
LANES = 256
STAGES = ((0, 8, 128), (8, 4, 64), (12, 4, 64))
UNROLL = 16
NEXT = ((3, 4), (5, 6), (7, 8))
MESH = pl.DeviceIdType.MESH
BF, F32 = jnp.bfloat16, jnp.float32
BIG = 1e30
TO_LOG2 = math.log2(math.e) / math.sqrt(HEAD_DIM)


def nt(a, b):
    return lax.dot_general(a, b, (((1,), (1,)), ((), ())), preferred_element_type=F32)


def nn(a, b):
    return jnp.dot(a, b, preferred_element_type=F32)


def iota(shape, dim):
    return lax.broadcasted_iota(jnp.int32, shape, dim)


def body(cols_ref, q_hbm, k_hbm, v_hbm, w_hbm, o_ref, zbuf, pbuf, ybuf, wts, obuf, rbuf, cbuf, abuf, home, wbuf,
         kvl, ssel, sz, sg, qb, ekey, perm, lsrc, lbuf, acc, mx, tot, own, xsend, xrecv,
         zss, zrs, gss, grs, pss, prs, rss, rrs, lss, lrs, ass, ars, xss, xrs, loc):
    me = lax.axis_index("rows")
    t = lax.axis_index("heads")
    c = lax.rem(me, 2)
    z = lax.rem(lax.div(me, 2), NZ)
    g = lax.div(me, 2 * NZ)
    p = g * 2 + c
    x, y_hi = lax.div(g, 2), lax.rem(g, 2)
    odd_x = lax.rem(x, 2)

    def row_id(gg, zz, cc):
        return (gg * NZ + zz) * 2 + cc

    def z_mate(s):
        zz = lax.rem(z + s, NZ)
        return zz, {"rows": row_id(g, zz, c)}

    def each_z_mate(act):
        @pl.loop(1, NZ // 2)
        def _(s):
            act(*z_mate(s))
            act(*z_mate(NZ - s))

        act(*z_mate(NZ // 2))

    def remote(src, dst, ssem, rsem, device):
        return pltpu.make_async_remote_copy(
            src_ref=src, dst_ref=dst, send_sem=ssem, recv_sem=rsem, device_id=device, device_id_type=MESH
        )

    def local(src, dst, sem):
        pltpu.make_async_copy(src, dst, sem).start()

    def drain(ref, sem):
        pltpu.make_async_copy(ref, ref, sem).wait()

    def owner(st, k):
        if st == 0:
            return k, 0
        return 2 * k + (lax.rem(k, 2) if st == 1 else 1 - lax.rem(k, 2)), 1

    def mine(st):
        if st == 0:
            return c == 0
        return (c == 1) & (y_hi == (odd_x if st == 1 else 1 - odd_x))

    def my_block(st):
        return g if st == 0 else x

    def stage_cols(st):
        return pl.ds(STAGES[st][0] * BLOCK, STAGES[st][2])

    hbm = (q_hbm, k_hbm, v_hbm)
    kv_loads = [pltpu.make_async_copy(hbm[1 + a], kvl.at[a], loc.at[a]) for a in range(2)]
    barrier = pltpu.get_barrier_semaphore()

    @pl.loop(1, NZ)
    def _(s):
        pl.semaphore_signal(barrier, inc=1, device_id=z_mate(s)[1], device_id_type=MESH)

    @pl.loop(1, 2 * NG)
    def _(s):
        d = lax.rem(p + s, 2 * NG)
        device = {"rows": row_id(lax.div(d, 2), z, lax.rem(d, 2))}
        pl.semaphore_signal(barrier, inc=1, device_id=device, device_id_type=MESH)

    pl.semaphore_signal(barrier, inc=1, device_id={"heads": 1 - t}, device_id_type=MESH)
    for load in kv_loads:
        load.start()
    w_load = pltpu.make_async_copy(w_hbm, wbuf, loc.at[2])

    def head_lanes(zz):
        return pl.ds(pl.multiple_of(zz * HEAD_DIM, HEAD_DIM), HEAD_DIM)

    chunks = 3 * len(STAGES)

    def start_chunk(ch):
        st, a = ch // 3, ch % 3
        rows = stage_cols(st)
        local(hbm[a].at[rows, head_lanes(z)], zbuf.at[a, z, rows], zrs.at[ch])

        @each_z_mate
        def _(zz, device):
            remote(hbm[a].at[rows, head_lanes(zz)], zbuf.at[a, z, rows], zss.at[ch], zrs.at[ch], device).start()

    def chunk_left(ch):
        drain(zbuf.at[ch % 3, pl.ds(0, NZ - 1), stage_cols(ch // 3)], zss.at[ch])

    pl.semaphore_wait(barrier, NZ - 1 + 2 * NG - 1 + 1)

    start_chunk(0)

    lane1 = iota((1, HEAD_DIM), 1)
    sub16 = iota((SUMS, COLS), 0)
    as_row = jnp.full((1, HEAD_DIM), -1, jnp.int32)
    as_col = jnp.full((SUMS, COLS), -1, jnp.int32)
    for j in range(SUMS):
        as_row = jnp.where(lane1 == j, cols_ref[j], as_row)
        as_col = jnp.where(sub16 == j, cols_ref[j], as_col)
    pick = jnp.where(iota((SUMS, COLS), 1) == as_col, 1.0, 0.0).astype(BF)
    for a, load in enumerate(kv_loads):
        load.wait()
        ssel[a] = nn(pick, kvl[a]).astype(BF)

    local(ssel.at[:, :, head_lanes(z)], sz.at[:, z], zrs.at[chunks])

    @each_z_mate
    def _(zz, device):
        remote(ssel.at[:, :, head_lanes(zz)], sz.at[:, z], zss.at[chunks], zrs.at[chunks], device).start()

    for ch in range(1, len(NEXT)):
        start_chunk(ch)
    w_load.start()

    lane = iota((COLS, HEAD_DIM), 1)
    not_own = jnp.where(iota((COLS, HEAD_DIM), 0) == as_row, -BIG, 0.0)
    for zz in range(NZ):
        pos = lane - SUMS
        kz, cc = pos % NZ, pos // NZ
        later = (kz > zz) | ((kz == zz) & (cc >= c))
        in_lanes = (pos >= 0) & (pos < 2 * NZ)
        qb[zz] = jnp.where(in_lanes & later, -BIG, not_own).astype(BF)
    key = iota((COLS, HEAD_DIM), 0)
    for_j = lane == key % SUMS
    for_row = lane == SUMS + key // SUMS
    ekey[0] = jnp.where(for_j, 1.0, 0.0).astype(BF)
    ekey[1] = jnp.where(for_j | for_row, 1.0, 0.0).astype(BF)
    out_i, in_i = iota((COLS, COLS), 0), iota((COLS, COLS), 1)
    perm[...] = jnp.where((out_i // 16 == in_i % 16) & (out_i % 16 == in_i // 16), 1.0, 0.0).astype(BF)
    eye = jnp.where(out_i == in_i, 1.0, 0.0).astype(BF)
    eye1 = eye[:HEAD_DIM, :HEAD_DIM]
    ones = jnp.ones((16, 2 * COLS), BF)
    acc[...] = jnp.zeros_like(acc)
    mx[...] = jnp.full_like(mx, -BIG)
    tot[...] = jnp.zeros_like(tot)

    def share_summary():
        drain(sz, zrs.at[chunks])
        local(sz, sg.at[c, :, g], grs.at[0])

        @pl.loop(1, NG)
        def _(s):
            remote(sz, sg.at[c, :, g], gss.at[0], grs.at[0], {"rows": row_id(lax.rem(g + s, NG), z, c)}).start()

    def share_summary_cores():
        drain(sg.at[c], grs.at[0])
        remote(sg.at[c], sg.at[c], gss.at[1], grs.at[1], {"rows": row_id(g, z, 1 - c)}).start()

    def forward(a, st):
        ch = st * 3 + a
        drain(zbuf.at[a, :, stage_cols(st)], zrs.at[ch])
        if ch < len(NEXT):
            chunk_left(ch)
            for later in NEXT[ch]:
                start_chunk(later)
        first, count, _w = STAGES[st]

        def part(k):
            return zbuf.at[a, :, pl.ds(pl.multiple_of((first + k) * BLOCK, BLOCK), BLOCK)]

        def send(k):
            gg, cc = owner(st, k)
            remote(part(k), pbuf.at[a, p], pss.at[a, st], prs.at[a], {"rows": row_id(gg, z, cc)}).start()

        k0 = my_block(st)

        @pl.loop(1, count)
        def _(s):
            send(lax.rem(k0 + s, count))

        @pl.when(mine(st))
        def _():
            local(part(k0), pbuf.at[a, p], prs.at[a])

        @pl.when(jnp.logical_not(mine(st)))
        def _():
            send(k0)

    def update(st, i, lanes, s, vt):
        old = mx[st, i, :1, lanes]
        new = jnp.maximum(old, jnp.max(s, axis=0, keepdims=True))
        shrink = jnp.exp2(old - new)
        got = nn(vt, jnp.exp2(s - new).astype(BF))
        acc[st, i, :, lanes] = acc[st, i, :, lanes] * shrink + got[:HEAD_DIM]
        tot[st, i, :1, lanes] = tot[st, i, :1, lanes] * shrink + got[HEAD_DIM : HEAD_DIM + 1]
        mx[st, i, :1, lanes] = new

    def static_cols(st):
        return slice(STAGES[st][0] * BLOCK, STAGES[st][0] * BLOCK + STAGES[st][2])

    def summary(st, part=0, parts=1):
        per = LANES // STAGES[st][2]

        @pl.loop(lax.div((g + 1) * part, parts), lax.div((g + 1) * (part + 1), parts))
        def _(gg):
            keys = jnp.concatenate([sg[cc, 0, gg].reshape(HEAD_DIM, HEAD_DIM) for cc in range(2)], axis=0)
            vals = jnp.concatenate([sg[cc, 1, gg].reshape(HEAD_DIM, HEAD_DIM) for cc in range(2)], axis=0)
            keys = jnp.concatenate([keys, ekey[(gg == g).astype(jnp.int32)]], axis=1)
            vt = jnp.concatenate([nt(eye1, vals).astype(BF), ones[:, :COLS]], axis=0)
            for i in range(NZ // per):
                rows = slice(per * i, per * i + per)
                qs = [r.reshape(LANES, HEAD_DIM) for r in (zbuf[0, rows, static_cols(st)], qb[rows, static_cols(st)])]
                update(st, i, slice(0, LANES), nt(keys, jnp.concatenate(qs, axis=1)) * TO_LOG2, vt)

    def near(st):
        width = STAGES[st][2]
        n = STAGES[st][0] * BLOCK + width
        per = HEAD_DIM // width
        ki, qi = iota((per * n, HEAD_DIM), 0), iota((per * n, HEAD_DIM), 1)
        before = ki % n if per == 1 else jnp.where(ki >= n, ki - n, ki)
        before = before < qi % width + STAGES[st][0] * BLOCK
        if per > 1:
            before = before & ((ki >= n) == (qi >= width))

        @pl.loop(0, NZ // per // 2)
        def _(i):
            for e in range(2):
                rows = pl.ds((2 * i + e) * per, per)
                s = nt(
                    zbuf[1, rows, :n].reshape(per * n, HEAD_DIM),
                    zbuf[0, rows, static_cols(st)].reshape(HEAD_DIM, HEAD_DIM),
                )
                s = jnp.where(before, s * TO_LOG2, -BIG)
                vt = nt(eye1, zbuf[2, rows, :n].reshape(per * n, HEAD_DIM)).astype(BF)
                vt = jnp.concatenate([vt, ones[:, : per * n]], axis=0)
                update(st, i, slice(e * HEAD_DIM, (e + 1) * HEAD_DIM), s, vt)

    sh = (HEAD_DIM, HEAD_DIM)

    def by_column(a):
        drain(pbuf.at[a], prs.at[a])

        @pl.loop(0, NG, unroll=NG)
        def _(gg):
            y = nn(perm[...], pbuf[a, pl.ds(2 * gg, 2)].reshape(COLS, HEAD_DIM))
            ybuf[a, :, gg] = y.astype(BF).reshape(BLOCK, 16, HEAD_DIM)

    def lse_lane(st, i):
        at = my_block(st) * BLOCK + i
        if STAGES[st][2] < HEAD_DIM:
            at = at + (iota(sh, 0) % 2) * STAGES[st][2]
        return iota(sh, 1) == at

    def column_weights(st):
        @pl.when(mine(st))
        def _():
            by_column(0)
            by_column(1)

            def row_of(i):
                return (i // 16) * 16 + (i % 8) * 2 + (i // 8) % 2

            causal = row_of(iota(sh, 1)) <= row_of(iota(sh, 0))
            lsrc[...] = jnp.zeros_like(lsrc)

            @pl.loop(0, BLOCK, unroll=UNROLL)
            def _(i):
                qc, kc = (ybuf[a, i].reshape(sh) for a in range(2))
                s = jnp.where(causal, nt(qc, kc) * TO_LOG2, -BIG)
                peak = jnp.max(s, axis=1, keepdims=True)
                wts[i] = jnp.exp2(s - peak).astype(BF)
                lsrc[...] = jnp.where(lse_lane(st, i), peak, lsrc[...])

    def column_values(st):
        first, count, _w = STAGES[st]

        @pl.when(mine(st))
        def _():
            by_column(2)
            one = jnp.ones(sh, BF)

            @pl.loop(0, BLOCK, unroll=UNROLL)
            def _(i):
                got = nn(wts[i], jnp.concatenate([ybuf[2, i].reshape(sh), one], axis=1))
                total = got[:, HEAD_DIM:]
                obuf[i] = (got[:, :HEAD_DIM] / total).astype(BF).reshape(NG, 16, HEAD_DIM)
                lsrc[...] = lsrc[...] + jnp.where(lse_lane(st, i), jnp.log2(total), 0.0)

            b = first + my_block(st)

            def give_back(gg):
                y = nn(perm[...], obuf[:, gg].reshape(COLS, HEAD_DIM))
                rbuf[pl.ds(2 * gg, 2)] = y.astype(BF).reshape(2, NZ, BLOCK, HEAD_DIM)

            def tile(d):
                return lsrc.at[pl.ds(pl.multiple_of(d * NZ, NZ), NZ)]

            def send_back(gg, cc):
                d = gg * 2 + cc
                device = {"rows": row_id(gg, z, cc)}
                remote(tile(d), lbuf.at[b], lss, lrs.at[st], device).start()
                remote(rbuf.at[d], cbuf.at[b], rss, rrs.at[st], device).start()

            @pl.loop(1, NG)
            def _(s):
                gg = lax.rem(g + s, NG)
                give_back(gg)
                for cc in range(2):
                    send_back(gg, cc)

            give_back(g)
            send_back(g, 1 - c)
            local(rbuf.at[p], cbuf.at[b], rrs.at[st])
            local(tile(p), lbuf.at[b], lrs.at[st])

    def merge(st):
        first, count, width = STAGES[st]
        drain(lbuf.at[pl.ds(first, count)], lrs.at[st])
        drain(cbuf.at[pl.ds(first, count)], rrs.at[st])
        lse_all = jnp.sum(lbuf[first : first + count], axis=0)
        per = LANES // width
        for i in range(NZ // per):
            rows = range(per * i, per * i + per)
            lse = [lse_all[zz : zz + 1] for zz in rows]
            if per > 2:
                lse = [lse[0] + lse[1], lse[2] + lse[3]]
            lse = jnp.concatenate(lse, axis=1)
            m = mx[st, i, :1]
            peak = jnp.maximum(m, lse)
            near_w = jnp.exp2(m - peak)
            col_w = jnp.exp2(lse - peak)
            inv = 1.0 / (tot[st, i, :1] * near_w + col_w)
            col = [cbuf[first : first + count, zz].reshape(width, HEAD_DIM) for zz in rows]
            col_t = nt(eye1, jnp.concatenate(col, axis=0))
            out_t = acc[st, i] * (near_w * inv) + col_t * (col_w * inv)
            out = nt(eye, out_t.astype(BF)).astype(BF)
            abuf[per * i : per * i + per, static_cols(st)] = out.reshape(per, width, HEAD_DIM)
        cols = stage_cols(st)
        local(abuf.at[z, cols], home.at[cols, head_lanes(z)], ars.at[st])

        @each_z_mate
        def _(zz, device):
            remote(abuf.at[zz, cols], home.at[cols, head_lanes(z)], ass.at[st], ars.at[st], device).start()

    width = NZ * HEAD_DIM

    def project(st):
        cols = stage_cols(st)
        drain(home.at[cols], ars.at[st])
        theirs = pl.ds(pl.multiple_of((1 - t) * width, width), width)
        ours = pl.ds(pl.multiple_of(t * width, width), width)
        xsend[cols] = nn(home[cols], wbuf[:, theirs]).astype(BF)
        remote(xsend.at[cols], xrecv.at[cols], xss.at[st], xrs.at[st], {"heads": 1 - t}).start()
        own[cols] = nn(home[cols], wbuf[:, ours])

    def finish(st):
        cols = stage_cols(st)
        drain(xrecv.at[cols], xrs.at[st])
        o_ref[cols] = (own[cols] + xrecv[cols].astype(F32)).astype(BF)

    Q, K, V = range(3)
    share_summary()
    forward(Q, 0)
    forward(K, 0)
    share_summary_cores()
    forward(V, 0)
    near(0)
    drain(sg.at[1 - c], grs.at[1])
    column_weights(0)
    forward(Q, 1)
    summary(0, 0, 2)
    forward(K, 1)
    column_values(0)
    forward(V, 1)
    summary(0, 1, 2)
    forward(Q, 2)
    column_weights(1)
    forward(K, 2)
    near(1)
    merge(0)
    column_values(1)
    forward(V, 2)
    column_weights(2)
    summary(1)
    column_values(2)
    merge(1)
    summary(2)
    near(2)
    w_load.wait()
    project(0)
    merge(2)
    project(1)
    finish(0)
    project(2)
    finish(1)
    finish(2)

    drain(sz.at[:, pl.ds(0, NZ - 1)], zss.at[chunks])
    drain(sg.at[0, :, pl.ds(0, NG - 1)], gss.at[0])
    drain(sg.at[c], gss.at[1])
    for ch in range(len(NEXT), chunks):
        chunk_left(ch)
    for st, (first, count, _w) in enumerate(STAGES):
        for a in range(3):

            @pl.when(mine(st))
            def _():
                drain(pbuf.at[a, pl.ds(0, count - 1)], pss.at[a, st])

            @pl.when(jnp.logical_not(mine(st)))
            def _():
                drain(pbuf.at[a, pl.ds(0, count)], pss.at[a, st])

        cols = stage_cols(st)
        drain(abuf.at[pl.ds(0, NZ - 1), cols], ass.at[st])
        drain(xsend.at[cols], xss.at[st])
    drain(rbuf.at[pl.ds(0, 2 * NG - 1)], rss)
    drain(lsrc.at[pl.ds(0, (2 * NG - 1) * NZ)], lss)


def on_device(queries, keys, values, summary_cols, w_out):
    width = queries.shape[1]
    any_space = pl.BlockSpec(memory_space=pl.ANY)
    dma = pltpu.SemaphoreType.DMA
    vmem = pltpu.VMEM
    e = HEAD_DIM
    n = len(STAGES)
    return pl.pallas_call(
        body,
        out_shape=jax.ShapeDtypeStruct(queries.shape, BF),
        in_specs=[pl.BlockSpec(memory_space=pltpu.SMEM)] + [any_space] * 4,
        out_specs=pl.BlockSpec(memory_space=pltpu.VMEM),
        scratch_shapes=[
            vmem((3, NZ, COLS, e), BF),
            vmem((3, 2 * NG, NZ, BLOCK, e), BF),
            vmem((3, BLOCK, NG, 16, e), BF),
            vmem((BLOCK, e, e), BF),
            vmem((BLOCK, NG, 16, e), BF),
            vmem((2 * NG, NZ, BLOCK, e), BF),
            vmem((2 * NG, NZ, BLOCK, e), BF),
            vmem((NZ, COLS, e), BF),
            vmem((COLS, width), BF),
            vmem(w_out.shape, BF),
            vmem((2, COLS, width), BF),
            vmem((2, SUMS, width), BF),
            vmem((2, NZ, SUMS, e), BF),
            vmem((2, 2, NG, NZ, SUMS, e), BF),
            vmem((NZ, COLS, e), BF),
            vmem((2, COLS, e), BF),
            vmem((COLS, COLS), BF),
            vmem((e, e), F32),
            vmem((2 * NG, NZ, e), F32),
            vmem((n, NZ // 2, e, LANES), F32),
            vmem((n, NZ // 2, 8, LANES), F32),
            vmem((n, NZ // 2, 8, LANES), F32),
            vmem((COLS, width), F32),
            vmem((COLS, width), BF),
            vmem((COLS, width), BF),
            dma((3 * n + 1,)), dma((3 * n + 1,)),
            dma((2,)), dma((2,)),
            dma((3, n)), dma((3,)),
            dma, dma((n,)),
            dma, dma((n,)),
            dma((n,)), dma((n,)),
            dma((n,)), dma((n,)),
            dma((3,)),
        ],
        name="strided_attention",
        compiler_params=pltpu.CompilerParams(
            collective_id=0, has_side_effects=True, vmem_limit_bytes=62 * 1024 * 1024
        ),
    )(summary_cols, queries, keys, values, w_out)


def solution(mesh):
    return jax.shard_map(
        on_device,
        mesh=mesh,
        in_specs=(P("rows", "heads"), P("rows", "heads"), P("rows", "heads"), P(), P("heads", None)),
        out_specs=P("rows", "heads"),
        check_vma=False,
    )
```

time: 108 us -> 84 us (0.78)
  the two profiles are of different devices: /device:TPU:1 before, /device:TPU:7 now
where the time goes in v2:
time: 84 us; the launch traced here: 83.9 us
  Pallas kernels  82 us (98%)
  local copies, waits for them, and re-layouts  1.87 us (2%)
    pallas_call x1, Pallas kernels, on_device(): pl.pallas_call(body, out_shape=jax.ShapeDtypeStruct(queries.shape, BF), i...  82 us
    unnamed x1, local copies, waits for them, and re-layouts  1.87 us

profile of v2, /device:TPU:7, one launch (start us, length us, event | category | flops | bytes accessed | tf_op | source)
XLA Modules:
  0.0 83.9 jit_solution(10882572655197550884)
XLA Ops:
  0.0 82.0 %strided_attention.1 = bf16[256,1024]{1,0:T(8,128)(2,1)} custom-call(s32[16]{0:T(128)} %cols_ref.1, bf16[256,1024]{1,0:T(8,128)(2,1)} %q_hbm.1, bf16[256,1024]{1,0:T(8,128)(2,1)} %k_hbm.1, bf16[256,1024]{1,0:T(8,128)(2,1)} %v_hbm.1, bf16[1024,2048]{1,0:T(8,128)(2,1)} %w_hbm.1), custom_call_target="tpu_custom_call" | custom-call | tf_op jit(solution)/shard_map/strided_attention/pallas_call | solution.py:457
  82.1 1.9 %copy.7 = bf16[256,1024]{1,0:T(8,128)(2,1)} copy(bf16[256,1024]{1,0:T(8,128)(2,1)} %strided_attention.1) | data formatting | bytes 1048576

commit v3 on v2

--- a/solution.py
+++ b/solution.py
@@ -16,7 +16,7 @@
 LANES = 256
 STAGES = ((0, 8, 128), (8, 4, 64), (12, 4, 64))
 UNROLL = 16
-NEXT = ((3, 4), (5, 6), (7, 8))
+NEXT = ((3,), (4,), (5,), (6,), (7,), (8,))
 MESH = pl.DeviceIdType.MESH
 BF, F32 = jnp.bfloat16, jnp.float32
 BIG = 1e30
@@ -36,7 +36,7 @@
 
 
 def body(cols_ref, q_hbm, k_hbm, v_hbm, w_hbm, o_ref, zbuf, pbuf, ybuf, wts, obuf, rbuf, cbuf, abuf, home, wbuf,
-         kvl, ssel, sz, sg, qb, ekey, perm, lsrc, lbuf, acc, mx, tot, own, xsend, xrecv,
+         kvl, ssel, sz, sg, qb, ekey, perm, lsrc, lbuf, acc, mx, tot, own, xsend, xrecv, res,
          zss, zrs, gss, grs, pss, prs, rss, rrs, lss, lrs, ass, ars, xss, xrs, loc):
     me = lax.axis_index("rows")
     t = lax.axis_index("heads")
@@ -76,15 +76,15 @@
     def owner(st, k):
         if st == 0:
             return k, 0
-        return 2 * k + (lax.rem(k, 2) if st == 1 else 1 - lax.rem(k, 2)), 1
+        return 4 * lax.div(k, 2) + 2 * (st - 1) + lax.rem(k, 2), 1
 
     def mine(st):
         if st == 0:
             return c == 0
-        return (c == 1) & (y_hi == (odd_x if st == 1 else 1 - odd_x))
+        return (c == 1) & (odd_x == st - 1)
 
     def my_block(st):
-        return g if st == 0 else x
+        return g if st == 0 else 2 * lax.div(x, 2) + y_hi
 
     def stage_cols(st):
         return pl.ds(STAGES[st][0] * BLOCK, STAGES[st][2])
@@ -124,10 +124,6 @@
 
     def chunk_left(ch):
         drain(zbuf.at[ch % 3, pl.ds(0, NZ - 1), stage_cols(ch // 3)], zss.at[ch])
-
-    pl.semaphore_wait(barrier, NZ - 1 + 2 * NG - 1 + 1)
-
-    start_chunk(0)
 
     lane1 = iota((1, HEAD_DIM), 1)
     sub16 = iota((SUMS, COLS), 0)
@@ -141,13 +137,15 @@
         load.wait()
         ssel[a] = nn(pick, kvl[a]).astype(BF)
 
+    pl.semaphore_wait(barrier, NZ - 1 + 2 * NG - 1 + 1)
+
     local(ssel.at[:, :, head_lanes(z)], sz.at[:, z], zrs.at[chunks])
 
     @each_z_mate
     def _(zz, device):
         remote(ssel.at[:, :, head_lanes(zz)], sz.at[:, z], zss.at[chunks], zrs.at[chunks], device).start()
 
-    for ch in range(1, len(NEXT)):
+    for ch in range(3):
         start_chunk(ch)
     w_load.start()
 
@@ -158,12 +156,13 @@
         kz, cc = pos % NZ, pos // NZ
         later = (kz > zz) | ((kz == zz) & (cc >= c))
         in_lanes = (pos >= 0) & (pos < 2 * NZ)
-        qb[zz] = jnp.where(in_lanes & later, -BIG, not_own).astype(BF)
+        qb[zz] = jnp.where((in_lanes & later) | (lane == 3 * SUMS), -BIG, not_own).astype(BF)
     key = iota((COLS, HEAD_DIM), 0)
     for_j = lane == key % SUMS
     for_row = lane == SUMS + key // SUMS
     ekey[0] = jnp.where(for_j, 1.0, 0.0).astype(BF)
     ekey[1] = jnp.where(for_j | for_row, 1.0, 0.0).astype(BF)
+    ekey[2] = jnp.where(lane == 3 * SUMS, 1.0, 0.0).astype(BF)
     out_i, in_i = iota((COLS, COLS), 0), iota((COLS, COLS), 1)
     perm[...] = jnp.where((out_i // 16 == in_i % 16) & (out_i % 16 == in_i // 16), 1.0, 0.0).astype(BF)
     eye = jnp.where(out_i == in_i, 1.0, 0.0).astype(BF)
@@ -229,13 +228,17 @@
 
     def summary(st, part=0, parts=1):
         per = LANES // STAGES[st][2]
-
-        @pl.loop(lax.div((g + 1) * part, parts), lax.div((g + 1) * (part + 1), parts))
-        def _(gg):
-            keys = jnp.concatenate([sg[cc, 0, gg].reshape(HEAD_DIM, HEAD_DIM) for cc in range(2)], axis=0)
-            vals = jnp.concatenate([sg[cc, 1, gg].reshape(HEAD_DIM, HEAD_DIM) for cc in range(2)], axis=0)
-            keys = jnp.concatenate([keys, ekey[(gg == g).astype(jnp.int32)]], axis=1)
-            vt = jnp.concatenate([nt(eye1, vals).astype(BF), ones[:, :COLS]], axis=0)
+        steps = lax.div(g + 2, 2)
+
+        @pl.loop(lax.div(steps * part, parts), lax.div(steps * (part + 1), parts))
+        def _(step):
+            both = [(2 * step + e, cc) for e in range(2) for cc in range(2)]
+            keys, vals = (
+                jnp.concatenate([sg[cc, a, gg].reshape(HEAD_DIM, HEAD_DIM) for gg, cc in both], axis=0) for a in range(2)
+            )
+            kind = [ekey[jnp.clip(2 * step + e - g + 1, 0, 2)] for e in range(2)]
+            keys = jnp.concatenate([keys, jnp.concatenate(kind, axis=0)], axis=1)
+            vt = jnp.concatenate([nt(eye1, vals).astype(BF), ones], axis=0)
             for i in range(NZ // per):
                 rows = slice(per * i, per * i + per)
                 qs = [r.reshape(LANES, HEAD_DIM) for r in (zbuf[0, rows, static_cols(st)], qb[rows, static_cols(st)])]
@@ -251,7 +254,7 @@
         if per > 1:
             before = before & ((ki >= n) == (qi >= width))
 
-        @pl.loop(0, NZ // per // 2)
+        @pl.loop(0, NZ // per // 2, unroll=NZ // per // 2)
         def _(i):
             for e in range(2):
                 rows = pl.ds((2 * i + e) * per, per)
@@ -385,42 +388,47 @@
     def finish(st):
         cols = stage_cols(st)
         drain(xrecv.at[cols], xrs.at[st])
-        o_ref[cols] = (own[cols] + xrecv[cols].astype(F32)).astype(BF)
+        res[cols] = (own[cols] + xrecv[cols].astype(F32)).astype(BF)
+        local(res.at[cols], o_ref.at[cols], loc.at[3 + st])
 
     Q, K, V = range(3)
     share_summary()
     forward(Q, 0)
+    share_summary_cores()
     forward(K, 0)
-    share_summary_cores()
+    drain(sg.at[1 - c], grs.at[1])
+    summary(0, 0, 4)
+    summary(0, 1, 4)
+    summary(0, 2, 4)
     forward(V, 0)
+    summary(0, 3, 4)
     near(0)
-    drain(sg.at[1 - c], grs.at[1])
+    forward(Q, 1)
     column_weights(0)
-    forward(Q, 1)
-    summary(0, 0, 2)
     forward(K, 1)
+    summary(1, 0, 2)
     column_values(0)
     forward(V, 1)
-    summary(0, 1, 2)
+    summary(1, 1, 2)
     forward(Q, 2)
     column_weights(1)
     forward(K, 2)
     near(1)
+    forward(V, 2)
+    column_values(1)
+    summary(2, 0, 2)
+    summary(2, 1, 2)
     merge(0)
-    column_values(1)
-    forward(V, 2)
     column_weights(2)
-    summary(1)
     column_values(2)
+    near(2)
     merge(1)
-    summary(2)
-    near(2)
     w_load.wait()
     project(0)
     merge(2)
     project(1)
+    project(2)
     finish(0)
-    project(2)
     finish(1)
     finish(2)
 
@@ -443,6 +451,7 @@
         cols = stage_cols(st)
         drain(abuf.at[pl.ds(0, NZ - 1), cols], ass.at[st])
         drain(xsend.at[cols], xss.at[st])
+        pltpu.make_async_copy(res.at[cols], o_ref.at[cols], loc.at[3 + st]).wait()
     drain(rbuf.at[pl.ds(0, 2 * NG - 1)], rss)
     drain(lsrc.at[pl.ds(0, (2 * NG - 1) * NZ)], lss)
 
@@ -458,7 +467,7 @@
         body,
         out_shape=jax.ShapeDtypeStruct(queries.shape, BF),
         in_specs=[pl.BlockSpec(memory_space=pltpu.SMEM)] + [any_space] * 4,
-        out_specs=pl.BlockSpec(memory_space=pltpu.VMEM),
+        out_specs=any_space,
         scratch_shapes=[
             vmem((3, NZ, COLS, e), BF),
             vmem((3, 2 * NG, NZ, BLOCK, e), BF),
@@ -475,7 +484,7 @@
             vmem((2, NZ, SUMS, e), BF),
             vmem((2, 2, NG, NZ, SUMS, e), BF),
             vmem((NZ, COLS, e), BF),
-            vmem((2, COLS, e), BF),
+            vmem((3, COLS, e), BF),
             vmem((COLS, COLS), BF),
             vmem((e, e), F32),
             vmem((2 * NG, NZ, e), F32),
@@ -485,6 +494,7 @@
             vmem((COLS, width), F32),
             vmem((COLS, width), BF),
             vmem((COLS, width), BF),
+            vmem((COLS, width), BF),
             dma((3 * n + 1,)), dma((3 * n + 1,)),
             dma((2,)), dma((2,)),
             dma((3, n)), dma((3,)),
@@ -492,11 +502,11 @@
             dma, dma((n,)),
             dma((n,)), dma((n,)),
             dma((n,)), dma((n,)),
-            dma((3,)),
+            dma((3 + n,)),
         ],
         name="strided_attention",
         compiler_params=pltpu.CompilerParams(
-            collective_id=0, has_side_effects=True, vmem_limit_bytes=62 * 1024 * 1024
+            collective_id=0, has_side_effects=True, vmem_limit_bytes=53 * 1024 * 1024
         ),
     )(summary_cols, queries, keys, values, w_out)
 

time: 84 us -> 77.8 us (0.926)
  the two profiles are of different devices: /device:TPU:7 before, /device:TPU:1 now
where the time goes in v3:
time: 77.8 us; the launch traced here: 76.8 us
  Pallas kernels  75.3 us (97%)
  local copies, waits for them, and re-layouts  1.45 us (2%)
    pallas_call x1, Pallas kernels, on_device(): pl.pallas_call(body, out_shape=jax.ShapeDtypeStruct(queries.shape, BF), i...  75.3 us

profile of v3, /device:TPU:1, one launch (start us, length us, event | category | flops | bytes accessed | tf_op | source)
XLA Modules:
  0.0 76.8 jit_solution(1985252520574219479)
XLA Ops:
  0.0 0.0 copy-start
  0.0 0.7 copy-done
  0.7 75.3 %strided_attention.1 = bf16[256,1024]{1,0:T(8,128)(2,1)S(1)} custom-call(s32[16]{0:T(128)S(1)} %copy-done, bf16[256,1024]{1,0:T(8,128)(2,1)} %q_hbm.1, bf16[256,1024]{1,0:T(8,128)(2,1)} %k_hbm.1, bf16[256,1024]{1,0:T(8,128)(2,1)} %v_hbm.1, bf16[1024,2048]{1,0:T(8,128)(2,1)} %w_hbm.1), custom_call_target="tpu_custom_call" | custom-call | tf_op jit(solution)/shard_map/strided_attention/pallas_call | solution.py:466
  76.0 0.8 %copy.7 = bf16[256,1024]{1,0:T(8,128)(2,1)} copy(bf16[256,1024]{1,0:T(8,128)(2,1)S(1)} %strided_attention.1) | data formatting | bytes 1048576
Async XLA Ops:
  0.0 0.7 copy-start

commit v4 on v3

--- a/solution.py
+++ b/solution.py
@@ -187,32 +187,33 @@
     def forward(a, st):
         ch = st * 3 + a
         drain(zbuf.at[a, :, stage_cols(st)], zrs.at[ch])
+        first, count, _w = STAGES[st]
+
+        def part(k):
+            return zbuf.at[a, :, pl.ds(pl.multiple_of((first + k) * BLOCK, BLOCK), BLOCK)]
+
+        def send(k):
+            gg, cc = owner(st, k)
+            remote(part(k), pbuf.at[a, p], pss.at[a, st], prs.at[a], {"rows": row_id(gg, z, cc)}).start()
+
+        k0 = my_block(st)
+
+        @pl.loop(1, count)
+        def _(s):
+            send(lax.rem(k0 + s, count))
+
+        @pl.when(mine(st))
+        def _():
+            local(part(k0), pbuf.at[a, p], prs.at[a])
+
+        @pl.when(jnp.logical_not(mine(st)))
+        def _():
+            send(k0)
+
         if ch < len(NEXT):
             chunk_left(ch)
             for later in NEXT[ch]:
                 start_chunk(later)
-        first, count, _w = STAGES[st]
-
-        def part(k):
-            return zbuf.at[a, :, pl.ds(pl.multiple_of((first + k) * BLOCK, BLOCK), BLOCK)]
-
-        def send(k):
-            gg, cc = owner(st, k)
-            remote(part(k), pbuf.at[a, p], pss.at[a, st], prs.at[a], {"rows": row_id(gg, z, cc)}).start()
-
-        k0 = my_block(st)
-
-        @pl.loop(1, count)
-        def _(s):
-            send(lax.rem(k0 + s, count))
-
-        @pl.when(mine(st))
-        def _():
-            local(part(k0), pbuf.at[a, p], prs.at[a])
-
-        @pl.when(jnp.logical_not(mine(st)))
-        def _():
-            send(k0)
 
     def update(st, i, lanes, s, vt):
         old = mx[st, i, :1, lanes]
@@ -322,7 +323,7 @@
 
             def give_back(gg):
                 y = nn(perm[...], obuf[:, gg].reshape(COLS, HEAD_DIM))
-                rbuf[pl.ds(2 * gg, 2)] = y.astype(BF).reshape(2, NZ, BLOCK, HEAD_DIM)
+                rbuf[2 * gg : 2 * gg + 2] = y.astype(BF).reshape(2, NZ, BLOCK, HEAD_DIM)
 
             def tile(d):
                 return lsrc.at[pl.ds(pl.multiple_of(d * NZ, NZ), NZ)]
@@ -333,14 +334,15 @@
                 remote(tile(d), lbuf.at[b], lss, lrs.at[st], device).start()
                 remote(rbuf.at[d], cbuf.at[b], rss, rrs.at[st], device).start()
 
+            for gg in range(NG):
+                give_back(gg)
+
             @pl.loop(1, NG)
             def _(s):
                 gg = lax.rem(g + s, NG)
-                give_back(gg)
                 for cc in range(2):
                     send_back(gg, cc)
 
-            give_back(g)
             send_back(g, 1 - c)
             local(rbuf.at[p], cbuf.at[b], rrs.at[st])
             local(tile(p), lbuf.at[b], lrs.at[st])
@@ -411,14 +413,14 @@
     forward(V, 1)
     summary(1, 1, 2)
     forward(Q, 2)
+    forward(K, 2)
     column_weights(1)
-    forward(K, 2)
     near(1)
     forward(V, 2)
     column_values(1)
     summary(2, 0, 2)
+    merge(0)
     summary(2, 1, 2)
-    merge(0)
     column_weights(2)
     column_values(2)
     near(2)

time: 77.8 us -> 77.1 us (level); the launches traced: 76.8 us -> 77 us
  no operation moved by 1% of the time
where the time goes in v4:
time: 77.1 us; the launch traced here: 77 us
  Pallas kernels  75.6 us (98%)
  local copies, waits for them, and re-layouts  1.45 us (2%)
    pallas_call x1, Pallas kernels, on_device(): pl.pallas_call(body, out_shape=jax.ShapeDtypeStruct(queries.shape, BF), i...  75.6 us

profile of v4, /device:TPU:1, one launch (start us, length us, event | category | flops | bytes accessed | tf_op | source)
XLA Modules:
  0.0 77.0 jit_solution(2855442397585304816)
XLA Ops:
  0.0 0.0 copy-start
  0.0 0.7 copy-done
  0.7 75.6 %strided_attention.1 = bf16[256,1024]{1,0:T(8,128)(2,1)S(1)} custom-call(s32[16]{0:T(128)S(1)} %copy-done, bf16[256,1024]{1,0:T(8,128)(2,1)} %q_hbm.1, bf16[256,1024]{1,0:T(8,128)(2,1)} %k_hbm.1, bf16[256,1024]{1,0:T(8,128)(2,1)} %v_hbm.1, bf16[1024,2048]{1,0:T(8,128)(2,1)} %w_hbm.1), custom_call_target="tpu_custom_call" | custom-call | tf_op jit(solution)/shard_map/strided_attention/pallas_call | solution.py:468
  76.2 0.8 %copy.7 = bf16[256,1024]{1,0:T(8,128)(2,1)} copy(bf16[256,1024]{1,0:T(8,128)(2,1)S(1)} %strided_attention.1) | data formatting | bytes 1048576
Async XLA Ops:
  0.0 0.7 copy-start

commit v5 on v4

--- a/solution.py
+++ b/solution.py
@@ -381,10 +381,14 @@
     def project(st):
         cols = stage_cols(st)
         drain(home.at[cols], ars.at[st])
-        theirs = pl.ds(pl.multiple_of((1 - t) * width, width), width)
         ours = pl.ds(pl.multiple_of(t * width, width), width)
-        xsend[cols] = nn(home[cols], wbuf[:, theirs]).astype(BF)
-        remote(xsend.at[cols], xrecv.at[cols], xss.at[st], xrs.at[st], {"heads": 1 - t}).start()
+        part = width // 2
+        for e in range(2):
+            theirs = pl.ds(pl.multiple_of((1 - t) * width + e * part, part), part)
+            lanes = pl.ds(e * part, part)
+            xsend[cols, lanes] = nn(home[cols], wbuf[:, theirs]).astype(BF)
+            src, dst = xsend.at[cols, lanes], xrecv.at[cols, lanes]
+            remote(src, dst, xss.at[st], xrs.at[st], {"heads": 1 - t}).start()
         own[cols] = nn(home[cols], wbuf[:, ours])
 
     def finish(st):

time: 77.1 us -> 76.9 us (level)
  no operation moved by 1% of the time
where the time goes in v5:
time: 76.9 us; the launch traced here: 76.8 us
  Pallas kernels  75.3 us (98%)
  local copies, waits for them, and re-layouts  1.45 us (2%)
    pallas_call x1, Pallas kernels, on_device(): pl.pallas_call(body, out_shape=jax.ShapeDtypeStruct(queries.shape, BF), i...  75.3 us

profile of v5, /device:TPU:1, one launch (start us, length us, event | category | flops | bytes accessed | tf_op | source)
XLA Modules:
  0.0 76.8 jit_solution(16520455519255603992)
XLA Ops:
  0.0 0.0 copy-start
  0.0 0.7 copy-done
  0.7 75.3 %strided_attention.1 = bf16[256,1024]{1,0:T(8,128)(2,1)S(1)} custom-call(s32[16]{0:T(128)S(1)} %copy-done, bf16[256,1024]{1,0:T(8,128)(2,1)} %q_hbm.1, bf16[256,1024]{1,0:T(8,128)(2,1)} %k_hbm.1, bf16[256,1024]{1,0:T(8,128)(2,1)} %v_hbm.1, bf16[1024,2048]{1,0:T(8,128)(2,1)} %w_hbm.1), custom_call_target="tpu_custom_call" | custom-call | tf_op jit(solution)/shard_map/strided_attention/pallas_call | solution.py:472
  76.0 0.8 %copy.7 = bf16[256,1024]{1,0:T(8,128)(2,1)} copy(bf16[256,1024]{1,0:T(8,128)(2,1)S(1)} %strided_attention.1) | data formatting | bytes 1048576
Async XLA Ops:
  0.0 0.7 copy-start
